TPU v7x, 128 devices: a whole 4x4x4 slice. The times are simulated.
128 devices in a mesh: lat: 8 (over x, core), lon: 16 (over y, z).
Axes of the slice: x: 4, y: 4, z: 4, core: 2. Of those that a mesh axis runs over, the one named last changes fastest.
Arguments:
- positions: int32 [9216], P(('lat', 'lon')), may hold values from 0 to 36863, as said below
- encoded: float32 [9216, 1280], P(('lat', 'lon')), may hold values from -6 to 6
- mask_token: float32 [1280], replicated, may hold values from -4 to 4
- norm_gain: float32 [1280], replicated, may hold values from 0.1 to 1.9
- w_query: float32 [1280, 640], replicated
- w_key: float32 [1280, 640], replicated
- w_value: float32 [1280, 640], replicated, may hold values from -0.15625 to 0.15625
- w_out: float32 [640, 1280], replicated, may hold values from -0.25 to 0.25
- cotangent: float32 [96, 384, 1280], P('lat', 'lon'), may hold values from -6 to 6
Outputs:
- decoded: float32 [96, 384, 1280], P('lat', 'lon')
- grad_query: float32 [1280, 640], P('lon')
- grad_key: float32 [1280, 640], P('lon')
- grad_value: float32 [1280, 640], P('lon')
- grad_out: float32 [640, 1280], P('lon')
- grad_mask: float32 [1280], P('lon')
- grad_gain: float32 [1280], P('lon')
- grad_encoded: float32 [9216, 1280], P(('lat', 'lon'))
Inputs may be any that keep to these rules, and one draw needn't show every extreme that they name: All positions are distinct cells, a quarter of the grid. Tile (a, b) is the block of 12 x (24) cells of index a along lat and b along lon. The 72 tokens of one encoder shard hold at most 2 cells of any one tile, and some tile holds exactly 2 from every shard.
All inputs are finite; a program needn't handle non-finite values.
Results may differ from a plain program's by a relative error of at most 0.0003.
Values sent between devices are 32-bit elements; how exact they have to be, the bound alone decides.
A program may use at most 192 MiB of HBM per device.

v0:
```python
import functools, math
import jax, jax.numpy as jnp
import numpy as np
from jax import lax
from jax.experimental import pallas as pl
from jax.experimental.pallas import tpu as pltpu
from jax.sharding import PartitionSpec as P

HEAD = 80
F32 = jnp.float32
BF16 = jnp.bfloat16


def split(x):
    hi = x.astype(BF16)
    return hi, (x - hi.astype(F32)).astype(BF16)


NN = (((1,), (0,)), ((), ()))
NT = (((1,), (1,)), ((), ()))
TN = (((0,), (0,)), ((), ()))


def dot(a, b, dims):
    return lax.dot_general(a, b, dims, preferred_element_type=F32)


def dot3(a, b, dims):
    return dot(a[0], b[0], dims) + (dot(a[0], b[1], dims) + dot(a[1], b[0], dims))


def head_lanes(h):
    low = h * HEAD // 128 * 128
    high = -(-(h + 1) * HEAD // 128) * 128
    return low, high


MESH = pl.DeviceIdType.MESH
SLOTS = 256
TROWS = 304
SHARD = 40
SCALE = 1.0 / 192.0


def tile_rows_map():
    def block(r0, c0, cols):
        return [(r0 + i) * 24 + c0 + j for i in range(6) for j in range(cols)]

    none = [-5] * 4
    order = block(6, 6, 12) + block(6, 18, 6) + none + block(0, 6, 12) + block(0, 18, 6) + none
    order += none + block(6, 0, 6) + none + block(0, 0, 6)
    return np.array(order, np.int32)


def split3(x):
    hi = x.astype(BF16)
    rest = x - hi.astype(F32)
    mid = rest.astype(BF16)
    return hi, mid, (rest - mid.astype(F32)).astype(BF16)


def pick(onehot, x, dims):
    hi, mid, lo = split3(x)
    return (dot(onehot, hi, dims) + dot(onehot, mid, dims)) + dot(onehot, lo, dims)


def onehot(cond):
    return jnp.where(cond, 1.0, 0.0).astype(BF16)


def swap_matrix():
    j = lax.broadcasted_iota(jnp.int32, (SLOTS, SLOTS), 0)
    i = lax.broadcasted_iota(jnp.int32, (SLOTS, SLOTS), 1)
    b = jnp.right_shift(j, 4)
    a = jnp.bitwise_and(jnp.right_shift(j, 1), 7)
    return onehot(i == a * 32 + b * 2 + jnp.bitwise_and(j, 1))


def flip_low(i):
    return i + 1 - 2 * (i % 2)


def flip_far(i):
    return 3 - i


def remote(src, dst, send, recv, device):
    copy = pltpu.make_async_remote_copy(
        src_ref=src, dst_ref=dst, send_sem=send, recv_sem=recv, device_id=device, device_id_type=MESH
    )
    copy.start()
    return copy


def rows_at(start, size):
    return pl.ds(pl.multiple_of(start, size), size)


def send_lon(src, dst, send, recv, a, b, lanes=None):
    cols = pl.ds(0, lanes or src.shape[1])
    copies = []
    for k in range(1, 16):
        peer = (b + k) % 16
        copies.append(remote(
            src.at[rows_at(peer * 16, 16), cols], dst.at[rows_at(b * 16, 16), cols], send.at[k - 1], recv.at[k - 1], (a, peer)
        ))
    dst[rows_at(b * 16, 16), :] = src[rows_at(b * 16, 16), :]
    return copies


def send_lat(src, dst, send, recv, a, b, lanes=None):
    cols = pl.ds(0, lanes or src.shape[1])
    copies = []
    for k in range(1, 8):
        peer = (a + k) % 8
        copies.append(remote(
            src.at[rows_at(peer * 32, 32), cols], dst.at[rows_at(a * 32, 32), cols], send.at[k - 1], recv.at[k - 1], (peer, b)
        ))
    dst[rows_at(a * 32, 32), :] = src[rows_at(a * 32, 32), :]
    return copies


def finish(copies):
    for copy in copies:
        copy.wait()


class Sum:
    def __init__(self, m, home, place, w, acc, r1, r2, r3, r4, r5, fin, send_sem, recv_sem):
        self.m, self.home, self.place = m, home, place
        self.w, self.acc, self.r = w, acc, (r1, r2, r3, r4, r5)
        self.fin, self.send_sem, self.recv_sem = fin, send_sem, recv_sem
        self.first = m % 2 == 0
        self.stage, self.slot, self.copies = 0, 0, []

    def chunk(self, i, half):
        rest = pl.ds(2 * half, 2)
        return (self.m, i, rest) if self.first else (self.m, rest, i)

    def piece(self, i, half):
        a, b, x, c, y, z = self.place
        rows = pl.ds(0, 24) if half == 0 else pl.ds(24, 16)
        return (self.m, y, i, rows) if self.first else (self.m, i, z, rows)

    def near(self, ring, i):
        a, b, x, c, y, z = self.place
        return (a, i * 4 + z) if ring == self.first else (a, y * 4 + i)

    def send(self, src, dst, device):
        k = self.slot
        self.slot += 1
        self.copies.append(remote(src, dst, self.send_sem.at[self.m, k], self.recv_sem.at[self.m, k], device))

    def begin(self):
        a, b, x, c, y, z = self.place
        m, acc, (r1, r2, r3, r4, r5) = self.m, self.acc, self.r
        me1, me2 = (y, z) if self.first else (z, y)
        s = self.stage
        if s == 0:
            self.send(self.w.at[self.home, :, :, 1 - c], acc.at[m], (a + 1 - 2 * c, b))
            return
        if s == 7:
            self.send(self.fin.at[m, c], self.fin.at[m, c], (a + 1 - 2 * c, b))
            return
        for half in range(2):
            q1, q2 = (flip_low, flip_far) if half == 0 else (flip_far, flip_low)
            rows = pl.ds(0, 24) if half == 0 else pl.ds(24, 16)
            if s == 1:
                p = q1(me1)
                self.send(acc.at[self.chunk(p, half)], r1.at[m, 0, half], self.near(True, p))
                self.send(acc.at[self.chunk(q2(p), half)], r1.at[m, 1, half], self.near(True, p))
            elif s == 2:
                p = q2(me1)
                self.send(acc.at[self.chunk(p, half)], r2.at[m, half], self.near(True, p))
            elif s == 3:
                p = q1(me2)
                self.send(acc.at[self.piece(p, half)], r3.at[m, 0, rows], self.near(False, p))
                self.send(acc.at[self.piece(q2(p), half)], r3.at[m, 1, rows], self.near(False, p))
            elif s == 4:
                p = q2(me2)
                self.send(acc.at[self.piece(p, half)], r4.at[m, rows], self.near(False, p))
            elif s == 5:
                self.send(acc.at[self.piece(me2, half)], r5.at[m, 0, rows], (q1(x) * 2 + c, b))
            elif s == 6:
                self.send(acc.at[self.piece(me2, half)], r5.at[m, 1, rows], (q2(x) * 2 + c, b))

    def end(self):
        a, b, x, c, y, z = self.place
        m, acc, (r1, r2, r3, r4, r5) = self.m, self.acc, self.r
        me1, me2 = (y, z) if self.first else (z, y)
        s = self.stage
        finish(self.copies)
        self.copies = []
        if s == 0:
            @pl.loop(0, 4)
            def _(i):
                acc[m, i] += self.w[self.home, i, :, c]
        for half in range(2):
            q2 = flip_far if half == 0 else flip_low
            rows = pl.ds(0, 24) if half == 0 else pl.ds(24, 16)
            if s == 1:
                acc[self.chunk(me1, half)] += r1[m, 0, half]
                acc[self.chunk(q2(me1), half)] += r1[m, 1, half]
            elif s == 2:
                acc[self.chunk(me1, half)] += r2[m, half]
            elif s == 3:
                acc[self.piece(me2, half)] += r3[m, 0, rows]
                acc[self.piece(q2(me2), half)] += r3[m, 1, rows]
            elif s == 4:
                acc[self.piece(me2, half)] += r4[m, rows]
            elif s == 5:
                acc[self.piece(me2, half)] += r5[m, 0, rows]
            elif s == 6:
                self.fin[m, c, rows] = (acc[self.piece(me2, half)] + r5[m, 1, rows]) * SCALE
        self.stage += 1

    def step(self):
        self.end()
        if self.stage < 8:
            self.begin()


def step_kernel(
    cell_ref, pos_ref, enc_ref, mask_ref, gain_ref, cot_hbm, wq_hbm, wk_hbm, wv_hbm, wo_hbm,
    decoded_hbm, dq_ref, dk_ref, dv_ref, do_ref, denc_ref, own_ref,
    w, w_hi, w_lo, o_hi, o_lo, acc, r1, r2, r3, r4, r5, fin, vr,
    tile_t, tile_g, land_t, land_g, sa0, ra0, rb0, sa1, ra1, rb1,
    t_ref, g_ref, xhat_ref, dn_ref, rstd_ref, n_hi, n_lo, qkv_ref, p_ref, att_ref, datt_ref, dqkv_ref,
    vec_ref, load_s, halo_s, halo_r, lon_s, lon_r, lat_s, lat_r, sum_s, sum_r, vec_s, vec_r, free_s,
):
    a, b = lax.axis_index("lat"), lax.axis_index("lon")
    x, c = a // 2, a % 2
    y, z = b // 4, b % 4
    rows, width = t_ref.shape
    inner = att_ref.shape[1]
    part = width // 2
    heads = inner // HEAD
    half = rows // 2
    up, right = (a + 1) % 8, (b + 1) % 16
    down, left = (a + 7) % 8, (b + 15) % 16

    load_cot = pltpu.make_async_copy(cot_hbm, xhat_ref, load_s.at[0])
    load_o = [
        pltpu.make_async_copy(wo_hbm.at[:, :, :, pl.ds(i * part, part)], w.at[0, :, :, i], load_s.at[1 + i])
        for i in range(2)
    ]
    load_v = pltpu.make_async_copy(wv_hbm, w.at[1], load_s.at[3])
    load_k = pltpu.make_async_copy(wk_hbm, w.at[0], load_s.at[4])
    load_q = pltpu.make_async_copy(wq_hbm, w.at[1], load_s.at[5])
    load_cot.start()
    load_o[0].start()
    load_o[1].start()
    load_v.start()

    def take_weight(load, home, which):
        load.wait()

        @pl.loop(0, 16)
        def _(i):
            r = pl.ds(pl.multiple_of(i * 80, 80), 80)
            cols = slice(which * inner, (which + 1) * inner)
            w_hi[r, cols], w_lo[r, cols] = split(w[home, i // 4, i % 4].reshape(80, inner))

    peers = [(a, (b + k) % 16) for k in range(1, 16)] + [((a + k) % 8, b) for k in range(1, 8)]
    peers += [(up, right), (down, left)]
    barrier = pltpu.get_barrier_semaphore()
    for peer in peers:
        pl.semaphore_signal(barrier, inc=1, device_id=peer, device_id_type=MESH)

    count = enc_ref.shape[0]
    pos = pos_ref[...].astype(F32)
    lat = jnp.floor((pos + 0.5) * (1.0 / 384.0))
    lon = pos - lat * 384.0
    tile_a = jnp.floor((lat + 0.5) * (1.0 / 12.0))
    tile_b = jnp.floor((lon + 0.5) * (1.0 / 24.0))
    cell = (lat - tile_a * 12.0) * 24.0 + lon - tile_b * 24.0
    target = tile_a * 16.0 + tile_b
    line = lax.broadcasted_iota(jnp.int32, (count, count), 0)
    lane = lax.broadcasted_iota(jnp.int32, (count, count), 1)

    def column(v):
        return jnp.sum(jnp.where(line == lane, v, 0.0), axis=1, keepdims=True)

    earlier = jnp.logical_and(column(target) == target, line < lane)
    rank = jnp.sum(jnp.where(earlier, 1.0, 0.0), axis=0, keepdims=True)
    index1 = target * 2.0 + rank
    index2 = tile_b * 16.0 + tile_a * 2.0 + rank
    column1, column2 = column(index1), column(index2)

    seats = lax.broadcasted_iota(jnp.int32, (SLOTS, count), 0).astype(F32)
    to2 = onehot(seats == index2)
    sa0[:, :part] = pick(to2, enc_ref[:, :part], NN)
    sa0[:, part:] = pick(to2, jnp.broadcast_to(column(cell) + 1.0, (count, 128)), NN)
    to1 = onehot(seats == index1)
    sa1[...] = pick(to1, enc_ref[:, part:], NN)

    pl.semaphore_wait(barrier, len(peers))
    go0 = send_lon(sa0, ra0, lon_s.at[0], lon_r.at[0], a, b)
    go1 = send_lat(sa1, ra1, lat_s.at[0], lat_r.at[0], a, b)

    def halo(tile, land, whole, first):
        moves = (
            (224, 40, land.at[pl.ds(0, 40)], (a, left)), (112, 72, whole.at[pl.ds(72, 72)], (down, b)),
            (184, 40, land.at[pl.ds(40, 40)], (down, b)), (264, 40, land.at[pl.ds(80, 40)], (down, left)),
        )
        return [
            remote(tile.at[pl.ds(row, size)], dst, halo_s.at[first + i], halo_r.at[first + i], device)
            for i, (row, size, dst, device) in enumerate(moves)
        ]

    def settle(tile, land, whole):
        whole[0:72, :] = tile[0:72, :]
        whole[144:180, :] = tile[72:108, :]
        whole[180:216, :] = land[4:40, :]
        whole[216:252, :] = land[40:76, :]
        whole[252:288, :] = land[84:120, :]

    def halo_back(src, tile, first):
        moves = (
            (72, 72, 112, (up, b)), (216, 40, 184, (up, b)), (176, 40, 224, (a, right)), (248, 40, 264, (up, right)),
        )
        copies = [
            remote(src.at[pl.ds(row, size)], tile.at[pl.ds(to, size)], halo_s.at[first + i], halo_r.at[first + i], device)
            for i, (row, size, to, device) in enumerate(moves)
        ]
        tile[0:72, :] = src[0:72, :]
        tile[72:112, :] = src[144:184, :]
        return copies

    place = onehot(lax.broadcasted_iota(jnp.int32, (rows, TROWS), 0) == cell_ref[...])
    load_cot.wait()
    for j in range(0, width, 256):
        tile_g[:, j:j + 256] = pick(place, xhat_ref[:, j:j + 256], TN)

    load_o[0].wait()
    load_o[1].wait()
    for i in range(2):
        for j in range(4):
            r = slice(j * 160, (j + 1) * 160)
            o_hi[i, r, :], o_lo[i, r, :] = split(w[0, j, :, i].reshape(160, part))
    load_k.start()
    take_weight(load_v, 1, 2)
    load_q.start()

    swap = swap_matrix()
    finish(go0)
    sa0[...] = pick(swap, ra0[...], TN)
    go0 = send_lat(sa0, rb0, lat_s.at[1], lat_r.at[1], a, b)
    finish(go1)
    sa1[...] = pick(swap, ra1[...], NN)
    go1 = send_lon(sa1, rb1, lon_s.at[1], lon_r.at[1], a, b)

    take_weight(load_k, 0, 1)
    take_weight(load_q, 1, 0)

    def out_weight(i):
        return o_hi[i], o_lo[i]

    finish(go0)
    table = onehot(rb0[:, part:part + 1] == (cell_ref[...] + 1).astype(F32))
    table2 = dot(swap, table, NN).astype(BF16)
    seen = jnp.sum(table.astype(F32), axis=0, keepdims=True)
    lead = lax.broadcasted_iota(jnp.int32, (16, 1), 0) == 0
    unseen = jnp.where(lead, 1.0 - seen, 0.0).astype(BF16)
    mask = jnp.broadcast_to(jnp.concatenate([mask_ref[i:i + 1, :] for i in range(10)], axis=1), (16, width))
    gain = jnp.concatenate([gain_ref[i:i + 1, :] for i in range(10)], axis=1)
    tile_t[:, :part] = pick(table, rb0[:, :part], TN) + pick(unseen, mask[:, :part], TN)
    finish(go1)
    tile_t[:, part:] = pick(table2, rb1[...], TN) + pick(unseen, mask[:, part:], TN)
    halo_t = halo(tile_t, land_t, t_ref, 4)
    finish(halo_t)
    halo_g = halo(tile_g, land_g, g_ref, 0)
    settle(tile_t, land_t, t_ref)

    step = 32

    @pl.loop(0, rows // step)
    def _(i):
        r = pl.ds(pl.multiple_of(i * step, step), step)
        t = t_ref[r, :]
        centred = t - jnp.mean(t, axis=-1, keepdims=True)
        rstd = lax.rsqrt(jnp.mean(centred * centred, axis=-1, keepdims=True) + 1e-5)
        xhat = centred * rstd
        xhat_ref[r, :] = xhat
        rstd_ref[r, :] = rstd
        n_hi[r, :], n_lo[r, :] = split(xhat * gain)

    @pl.loop(0, 3 * inner // 256)
    def _(j):
        cols = pl.ds(pl.multiple_of(j * 256, 256), 256)
        qkv_ref[:, cols] = dot3((n_hi[...], n_lo[...]), (w_hi[:, cols], w_lo[:, cols]), NN)

    qkv_ref[:, 1792:] = dot3((n_hi[...], n_lo[...]), (w_hi[:, 1792:], w_lo[:, 1792:]), NN)

    finish(halo_g)
    settle(tile_g, land_g, g_ref)

    for peer in peers:
        pl.semaphore_signal(free_s, inc=1, device_id=peer, device_id_type=MESH)

    datt_ref[...] = dot3(split(g_ref[:, :part]), out_weight(0), NT)
    datt_ref[...] += dot3(split(g_ref[:, part:]), out_weight(1), NT)

    att_ref[...] = jnp.zeros_like(att_ref)
    dqkv_ref[...] = jnp.zeros_like(dqkv_ref)
    is_last = a == 7
    low_q = lax.broadcasted_iota(jnp.int32, (half, half), 0) >= half // 2
    low_k = lax.broadcasted_iota(jnp.int32, (half, half), 1) >= half // 2
    blocked = jnp.logical_and(low_q != low_k, is_last)
    norm = 1.0 / math.sqrt(HEAD)

    def head(h):
        lo, hi = head_lanes(h)
        lane = lax.broadcasted_iota(jnp.int32, (half, hi - lo), 1) + lo
        return lo, hi, jnp.logical_and(lane >= h * HEAD, lane < (h + 1) * HEAD)

    @pl.loop(0, 2)
    def _(wd):
        r = pl.ds(pl.multiple_of(wd * half, 16), half)
        for h in range(heads):
            lo, hi, mine = head(h)
            q = split(jnp.where(mine, qkv_ref[r, lo:hi] * norm, 0.0))
            k = split(qkv_ref[r, inner + lo:inner + hi])
            v = split(qkv_ref[r, 2 * inner + lo:2 * inner + hi])
            do = split(jnp.where(mine, datt_ref[r, lo:hi], 0.0))
            s = dot3(q, k, NT)
            s = jnp.where(blocked, -1e30, s)
            e = jnp.exp(s - jnp.max(s, axis=-1, keepdims=True))
            p32 = e / jnp.sum(e, axis=-1, keepdims=True)
            p_ref[wd * heads + h] = p32
            p = split(p32)
            att_ref[r, lo:hi] += jnp.where(mine, dot3(p, v, NN), 0.0)
            dqkv_ref[r, 2 * inner + lo:2 * inner + hi] += dot3(p, do, TN)

    att = split(att_ref[...])
    for i in range(2):
        t_ref[:, i * part:(i + 1) * part] += dot3(att, out_weight(i), NN)
    pl.semaphore_wait(free_s, len(peers))
    halo_o = halo_back(t_ref, tile_g, 12)

    sums = [
        Sum(m, m % 2, (a, b, x, c, y, z), w, acc, r1, r2, r3, r4, r5, fin, sum_s, sum_r) for m in range(4)
    ]

    att3 = jnp.concatenate([att[0], att[0], att[1]], axis=0)
    for i in range(2):
        gh, gl = split(g_ref[:, i * part:(i + 1) * part])
        res = dot(att3, jnp.concatenate([gh, gl, gh], axis=0), TN)
        w[0, :, :, i] = res.reshape(4, 4, SHARD, inner)
    sums[0].begin()

    def grad_rows(which):
        return split(dqkv_ref[:, which * inner:(which + 1) * inner])

    def to_tokens(which, dh, dl, add):
        d3 = jnp.concatenate([dh, dh, dl], axis=1)
        cols = slice(which * inner, (which + 1) * inner)
        for lo in range(0, width, 256):
            r = slice(lo, lo + 256)
            wh, wl = w_hi[r, cols], w_lo[r, cols]
            res = dot(d3, jnp.concatenate([wh, wl, wh], axis=1), NT)
            dn_ref[:, r] = dn_ref[:, r] + res if add else res

    def to_weight(which, dh, dl):
        d3 = jnp.concatenate([dh, dl, dh], axis=0)
        for i in range(2):
            cols = slice(i * part, (i + 1) * part)
            nh, nl = n_hi[:, cols], n_lo[:, cols]
            res = dot(jnp.concatenate([nh, nh, nl], axis=0), d3, TN)
            w[(3 - which) % 2, 2 * i:2 * i + 2] = res.reshape(2, 4, 2, SHARD, inner)

    dh, dl = grad_rows(2)
    to_weight(2, dh, dl)
    sums[1].begin()
    sums[0].step()
    to_tokens(2, dh, dl, False)
    sums[1].step()

    @pl.loop(0, 2)
    def _(wd):
        r = pl.ds(pl.multiple_of(wd * half, 16), half)
        for h in range(heads):
            lo, hi, mine = head(h)
            q = split(jnp.where(mine, qkv_ref[r, lo:hi] * norm, 0.0))
            k = split(qkv_ref[r, inner + lo:inner + hi])
            v = split(qkv_ref[r, 2 * inner + lo:2 * inner + hi])
            do = split(jnp.where(mine, datt_ref[r, lo:hi], 0.0))
            p32 = p_ref[wd * heads + h]
            dp = dot3(do, v, NT)
            ds = split(p32 * (dp - jnp.sum(dp * p32, axis=-1, keepdims=True)))
            dqkv_ref[r, lo:hi] += jnp.where(mine, dot3(ds, k, NN) * norm, 0.0)
            dqkv_ref[r, inner + lo:inner + hi] += dot3(ds, q, TN)

    kh, kl = grad_rows(1)
    to_weight(1, kh, kl)
    sums[2].begin()
    sums[0].step()
    qh, ql = grad_rows(0)
    to_weight(0, qh, ql)
    sums[3].begin()
    sums[2].step()
    sums[1].step()
    to_tokens(1, kh, kl, True)
    sums[3].step()
    sums[0].step()
    to_tokens(0, qh, ql, True)
    sums[1].step()

    vec_ref[...] = jnp.zeros_like(vec_ref)

    @pl.loop(0, rows // step)
    def _(i):
        r = pl.ds(pl.multiple_of(i * step, step), step)
        dn = dn_ref[r, :]
        xhat = xhat_ref[r, :]
        vec_ref[1:2, :] += jnp.sum(dn * xhat, axis=0, keepdims=True)
        dx = dn * gain
        m1 = jnp.mean(dx, axis=-1, keepdims=True)
        m2 = jnp.mean(dx * xhat, axis=-1, keepdims=True)
        g_ref[r, :] += rstd_ref[r, :] * (dx - m1 - xhat * m2)

    halo_d = halo_back(g_ref, tile_t, 8)

    sums[0].step()
    sums[1].step()

    finish(halo_o)
    for j in range(0, width, 256):
        xhat_ref[:, j:j + 256] = pick(place, tile_g[:, j:j + 256], NN)
    store = pltpu.make_async_copy(xhat_ref, decoded_hbm, load_s.at[0])
    store.start()
    sums[2].step()
    sums[3].step()

    finish(halo_d)
    sa1[...] = pick(table, tile_t[:, :part], NN)
    back0 = send_lat(sa1, ra1, lat_s.at[2], lat_r.at[2], a, b)
    sa0[:, :part] = pick(table2, tile_t[:, part:], NN)
    back1 = send_lon(sa0, ra0, lon_s.at[2], lon_r.at[2], a, b, part)
    masked = jnp.where(cell_ref[...] >= 0, 1.0 - seen, 0.0)
    masked = jnp.where(lead, masked, 0.0)[:8].astype(BF16)
    vec_ref[...] += pick(masked, tile_t[...], NN)

    vec_devices = [
        (a + 1 - 2 * c, b), (flip_low(x) * 2 + c, b), (flip_far(x) * 2 + c, b),
        (a, flip_low(y) * 4 + z), (a, flip_far(y) * 4 + z), (a, y * 4 + flip_low(z)), (a, y * 4 + flip_far(z)),
    ]
    vec_copies = []

    def vec_begin(k):
        vec_copies.append(remote(vec_ref, vr.at[k], vec_s.at[k], vec_r.at[k], vec_devices[k]))

    def vec_step():
        k = len(vec_copies) - 1
        vec_copies[k].wait()
        vec_ref[...] += vr[k]
        if k < 6:
            vec_begin(k + 1)

    vec_begin(0)
    sums[0].step()
    sums[1].step()
    sums[2].step()
    sums[3].step()
    vec_step()

    finish(back0)
    sa1[...] = pick(swap, ra1[...], NN)
    back0 = send_lon(sa1, rb1, lon_s.at[3], lon_r.at[3], a, b)
    finish(back1)
    sa0[:, :part] = pick(swap, ra0[:, :part], TN)
    back1 = send_lat(sa0, rb0, lat_s.at[3], lat_r.at[3], a, b, part)

    for _ in range(2):
        for total in sums:
            if total.stage < 8:
                total.step()
        vec_step()

    finish(back0)
    finish(back1)
    slots = lax.broadcasted_iota(jnp.int32, (count, SLOTS), 1).astype(F32)
    denc_ref[:, :part] = pick(onehot(slots == column2), rb1[...], NN)
    denc_ref[:, part:] = pick(onehot(slots == column1), rb0[:, :part], NN)

    while any(total.stage < 8 for total in sums):
        front = min(total.stage for total in sums)
        for total in sums:
            if total.stage == front:
                total.step()
        if len(vec_copies) < 7:
            vec_step()
    while len(vec_copies) < 7:
        vec_step()
    vec_step()
    lanes = lax.broadcasted_iota(jnp.int32, (width, 128), 1)
    mine = jnp.logical_and(lax.broadcasted_iota(jnp.int32, (width, 128), 0) == b * 80 + lanes, lanes < 80)
    mine = onehot(mine)
    hi, mid, lo = split3(vec_ref[...] * SCALE)
    own_ref[...] = (dot(hi, mine, NN) + dot(mid, mine, NN)) + dot(lo, mine, NN)
    do_ref[:, :part] = fin[0, 0]
    do_ref[:, part:] = fin[0, 1]
    dv_ref[...] = fin[1]
    dk_ref[...] = fin[2]
    dq_ref[...] = fin[3]
    store.wait()


def decoder_step(cell, pos, enc, mask, gain, cot, wq, wk, wv, wo):
    rows, width = cot.shape
    part = width // 2
    inner = wo.shape[2] * 16
    vm = pl.BlockSpec(memory_space=pltpu.VMEM)
    anyspace = pl.BlockSpec(memory_space=pl.ANY)
    f = jax.ShapeDtypeStruct
    dma = pltpu.SemaphoreType.DMA
    v = pltpu.VMEM
    third = f((2, SHARD, inner), F32)
    return pl.pallas_call(
        step_kernel,
        out_shape=(
            f((rows, width), F32), third, third, third, f((SHARD, width), F32), f((enc.shape[0], width), F32),
            f((8, 128), F32),
        ),
        in_specs=[vm] * 5 + [anyspace] * 5,
        out_specs=[anyspace] + [vm] * 6,
        scratch_shapes=[
            v((2, 4, 4, 2, SHARD, inner), F32), v((width, 3 * inner), BF16), v((width, 3 * inner), BF16),
            v((2, inner, part), BF16), v((2, inner, part), BF16), v((4, 4, 4, SHARD, inner), F32),
            v((4, 2, 2, 2, SHARD, inner), F32), v((4, 2, 2, SHARD, inner), F32),
            v((4, 2, SHARD, inner), F32), v((4, SHARD, inner), F32), v((4, 2, SHARD, inner), F32),
            v((4, 2, SHARD, inner), F32), v((7, 8, width), F32),
            v((TROWS, width), F32), v((TROWS, width), F32), v((120, width), F32), v((120, width), F32),
            v((SLOTS, part + 128), F32), v((SLOTS, part + 128), F32), v((SLOTS, part + 128), F32),
            v((SLOTS, part), F32), v((SLOTS, part), F32), v((SLOTS, part), F32),
            v((rows, width), F32), v((rows, width), F32), v((rows, width), F32), v((rows, width), F32),
            v((rows, 1), F32), v((rows, width), BF16), v((rows, width), BF16),
            v((rows, 3 * inner), F32), v((2 * inner // HEAD, rows // 2, rows // 2), F32),
            v((rows, inner), F32), v((rows, inner), F32), v((rows, 3 * inner), F32),
            v((8, width), F32), dma((6,)), dma((16,)), dma((16,)), dma((4, 15)), dma((4, 15)), dma((4, 7)), dma((4, 7)),
            dma((4, 18)), dma((4, 18)), dma((7,)), dma((7,)), pltpu.SemaphoreType.REGULAR,
        ],
        compiler_params=pltpu.CompilerParams(
            vmem_limit_bytes=63 * 2**20, collective_id=0, has_side_effects=True
        ),
        name="decoder_step",
    )(cell, pos, enc, mask, gain, cot, wq, wk, wv, wo)


def copy_kernel(*refs):
    ins, outs, sems = refs[:6], refs[7:13], refs[15]
    copies = [pltpu.make_async_copy(i, o, sems.at[k]) for k, (i, o) in enumerate(zip(ins, outs))]
    for copy in copies:
        copy.start()
    refs[13][...] = refs[6][0:1, :80].reshape(80)
    refs[14][...] = refs[6][1:2, :80].reshape(80)
    for copy in copies:
        copy.wait()


def hand_over(arrays, own):
    vm = pl.BlockSpec(memory_space=pltpu.VMEM)
    anyspace = pl.BlockSpec(memory_space=pl.ANY)
    short = jax.ShapeDtypeStruct((80,), F32)
    return pl.pallas_call(
        copy_kernel,
        out_shape=tuple(jax.ShapeDtypeStruct(x.shape, x.dtype) for x in arrays) + (short, short),
        in_specs=[anyspace] * 6 + [vm],
        out_specs=[anyspace] * 6 + [vm] * 2,
        scratch_shapes=[pltpu.SemaphoreType.DMA((6,))],
        compiler_params=pltpu.CompilerParams(vmem_limit_bytes=60 * 2**20),
        name="hand_over",
    )(*arrays, own)


def body(positions, encoded, mask_token, norm_gain, w_query, w_key, w_value, w_out, cotangent):
    model_width = encoded.shape[1]
    inner = w_out.shape[0]
    shard = (4, 4, 2, SHARD, inner)
    tile_map = jnp.asarray(tile_rows_map())[None]
    *arrays, own = decoder_step(
        tile_map, positions[None], encoded, mask_token.reshape(-1, 128), norm_gain.reshape(-1, 128),
        cotangent.reshape(-1, model_width), w_query.reshape(shard), w_key.reshape(shard),
        w_value.reshape(shard), w_out.reshape(4, 4, SHARD, model_width),
    )
    decoded, grad_query, grad_key, grad_value, grad_out, grad_encoded, grad_mask, grad_gain = hand_over(arrays, own)
    matrices = (g.reshape(-1, inner) for g in (grad_query, grad_key, grad_value))
    return (decoded.reshape(cotangent.shape), *matrices, grad_out, grad_mask, grad_gain, grad_encoded)


def solution(mesh):
    return jax.shard_map(
        body,
        mesh=mesh,
        in_specs=(
            P(("lat", "lon")),
            P(("lat", "lon"), None),
            P(),
            P(),
            P(),
            P(),
            P(),
            P(),
            P("lat", "lon", None),
        ),
        out_specs=(
            P("lat", "lon", None),
            P("lon", None),
            P("lon", None),
            P("lon", None),
            P("lon", None),
            P("lon"),
            P("lon"),
            P(("lat", "lon"), None),
        ),
        check_vma=False,
    )
```

profile of v0, /device:TPU:0, one launch (start us, length us, event | category | flops | bytes accessed | tf_op | source)
XLA Modules:
  0.0 250.2 jit_solution(1667303971067526126)
XLA Ops:
  0.6 166.4 %decoder_step.1 = (f32[288,1280]{1,0:T(8,128)}, f32[2,40,640]{2,1,0:T(8,128)}, f32[2,40,640]{2,1,0:T(8,128)}, f32[2,40,640]{2,1,0:T(8,128)}, f32[40,1280]{1,0:T(...) custom-call(s32[1,304]{1,0:T(1,128)} %constant.6.cell_ref, s32[1,72]{1,0:T(1,128)} %bitcast.19, f32[72,1280]{1,0:T(8,128)} %enc_ref.1, ...), custom_call_target="tpu_custom_call" | custom-call | tf_op jit(solution)/shard_map/decoder_step/pallas_call | solution.py:619
  167.0 83.0 %hand_over.1 = (f32[288,1280]{1,0:T(8,128)}, f32[2,40,640]{2,1,0:T(8,128)}, f32[2,40,640]{2,1,0:T(8,128)}, f32[2,40,640]{2,1,0:T(8,128)}, f32[40,1280]{1,0:T(8,1...) custom-call(f32[288,1280]{1,0:T(8,128)} %get-tuple-element.23.refs_0_, f32[2,40,640]{2,1,0:T(8,128)} %get-tuple-element.24.refs_1_, ...), custom_call_target="tpu_custom_call" | custom-call | tf_op jit(solution)/shard_map/hand_over/pallas_call | solution.py:665
where the time goes:
time: 251 us; the launch traced here: 250 us
  Pallas kernels  249 us (99%)
    pallas_call x1, Pallas kernels, decoder_step(): pl.pallas_call(step_kernel, out_shape=(f((rows, width), F32), third, thir...  166 us
    pallas_call x1, Pallas kernels, hand_over(): pl.pallas_call(copy_kernel, out_shape=tuple((jax.ShapeDtypeStruct(x.shape...  83 us

commit v1 on v0

--- a/solution.py
+++ b/solution.py
@@ -315,17 +315,21 @@
         whole[216:252, :] = land[40:76, :]
         whole[252:288, :] = land[84:120, :]
 
-    def halo_back(src, tile, first):
+    def halo_back(src, tile, first, cols):
         moves = (
             (72, 72, 112, (up, b)), (216, 40, 184, (up, b)), (176, 40, 224, (a, right)), (248, 40, 264, (up, right)),
         )
-        copies = [
-            remote(src.at[pl.ds(row, size)], tile.at[pl.ds(to, size)], halo_s.at[first + i], halo_r.at[first + i], device)
+        return [
+            remote(
+                src.at[pl.ds(row, size), cols], tile.at[pl.ds(to, size), cols],
+                halo_s.at[first + i], halo_r.at[first + i], device,
+            )
             for i, (row, size, to, device) in enumerate(moves)
         ]
+
+    def keep_own(src, tile):
         tile[0:72, :] = src[0:72, :]
         tile[72:112, :] = src[144:184, :]
-        return copies
 
     place = onehot(lax.broadcasted_iota(jnp.int32, (rows, TROWS), 0) == cell_ref[...])
     load_cot.wait()
@@ -337,7 +341,8 @@
     for i in range(2):
         for j in range(4):
             r = slice(j * 160, (j + 1) * 160)
-            o_hi[i, r, :], o_lo[i, r, :] = split(w[0, j, :, i].reshape(160, part))
+            cols = slice(i * part, (i + 1) * part)
+            o_hi[r, cols], o_lo[r, cols] = split(w[0, j, :, i].reshape(160, part))
     load_k.start()
     take_weight(load_v, 1, 2)
     load_q.start()
@@ -352,9 +357,6 @@
 
     take_weight(load_k, 0, 1)
     take_weight(load_q, 1, 0)
-
-    def out_weight(i):
-        return o_hi[i], o_lo[i]
 
     finish(go0)
     table = onehot(rb0[:, part:part + 1] == (cell_ref[...] + 1).astype(F32))
@@ -398,8 +400,7 @@
     for peer in peers:
         pl.semaphore_signal(free_s, inc=1, device_id=peer, device_id_type=MESH)
 
-    datt_ref[...] = dot3(split(g_ref[:, :part]), out_weight(0), NT)
-    datt_ref[...] += dot3(split(g_ref[:, part:]), out_weight(1), NT)
+    datt_ref[...] = dot3(split(g_ref[...]), (o_hi[...], o_lo[...]), NT)
 
     att_ref[...] = jnp.zeros_like(att_ref)
     dqkv_ref[...] = jnp.zeros_like(dqkv_ref)
@@ -433,20 +434,27 @@
             dqkv_ref[r, 2 * inner + lo:2 * inner + hi] += dot3(p, do, TN)
 
     att = split(att_ref[...])
-    for i in range(2):
-        t_ref[:, i * part:(i + 1) * part] += dot3(att, out_weight(i), NN)
+    att_row = jnp.concatenate([att[0], att[0], att[1]], axis=1)
+
+    @pl.loop(0, width // 256)
+    def _(j):
+        cols = pl.ds(pl.multiple_of(j * 256, 256), 256)
+        oh, ol = o_hi[:, cols], o_lo[:, cols]
+        t_ref[:, cols] += dot(att_row, jnp.concatenate([oh, ol, oh], axis=0), NN)
+
     pl.semaphore_wait(free_s, len(peers))
-    halo_o = halo_back(t_ref, tile_g, 12)
+    halo_o = halo_back(t_ref, tile_g, 12, pl.ds(0, width))
+    keep_own(t_ref, tile_g)
 
     sums = [
         Sum(m, m % 2, (a, b, x, c, y, z), w, acc, r1, r2, r3, r4, r5, fin, sum_s, sum_r) for m in range(4)
     ]
 
     att3 = jnp.concatenate([att[0], att[0], att[1]], axis=0)
+    gh, gl = split(g_ref[...])
+    res = dot(att3, jnp.concatenate([gh, gl, gh], axis=0), TN)
     for i in range(2):
-        gh, gl = split(g_ref[:, i * part:(i + 1) * part])
-        res = dot(att3, jnp.concatenate([gh, gl, gh], axis=0), TN)
-        w[0, :, :, i] = res.reshape(4, 4, SHARD, inner)
+        w[0, :, :, i] = res[:, i * part:(i + 1) * part].reshape(4, 4, SHARD, part)
     sums[0].begin()
 
     def grad_rows(which):
@@ -461,18 +469,21 @@
             res = dot(d3, jnp.concatenate([wh, wl, wh], axis=1), NT)
             dn_ref[:, r] = dn_ref[:, r] + res if add else res
 
-    def to_weight(which, dh, dl):
+    def to_weight(cols, homes):
+        dh, dl = split(dqkv_ref[:, cols])
         d3 = jnp.concatenate([dh, dl, dh], axis=0)
         for i in range(2):
-            cols = slice(i * part, (i + 1) * part)
-            nh, nl = n_hi[:, cols], n_lo[:, cols]
+            half = slice(i * part, (i + 1) * part)
+            nh, nl = n_hi[:, half], n_lo[:, half]
             res = dot(jnp.concatenate([nh, nh, nl], axis=0), d3, TN)
-            w[(3 - which) % 2, 2 * i:2 * i + 2] = res.reshape(2, 4, 2, SHARD, inner)
-
-    dh, dl = grad_rows(2)
-    to_weight(2, dh, dl)
+            for j, home in enumerate(homes):
+                block = res[:, j * inner:(j + 1) * inner]
+                w[home, 2 * i:2 * i + 2] = block.reshape(2, 4, 2, SHARD, inner)
+
+    to_weight(slice(2 * inner, 3 * inner), (1,))
     sums[1].begin()
     sums[0].step()
+    dh, dl = grad_rows(2)
     to_tokens(2, dh, dl, False)
     sums[1].step()
 
@@ -491,19 +502,18 @@
             dqkv_ref[r, lo:hi] += jnp.where(mine, dot3(ds, k, NN) * norm, 0.0)
             dqkv_ref[r, inner + lo:inner + hi] += dot3(ds, q, TN)
 
+    to_weight(slice(0, 2 * inner), (1, 0))
+    sums[2].begin()
+    sums[3].begin()
+    sums[0].step()
+    sums[1].step()
     kh, kl = grad_rows(1)
-    to_weight(1, kh, kl)
-    sums[2].begin()
+    to_tokens(1, kh, kl, True)
+    sums[2].step()
+    sums[3].step()
+    qh, ql = grad_rows(0)
+    to_tokens(0, qh, ql, True)
     sums[0].step()
-    qh, ql = grad_rows(0)
-    to_weight(0, qh, ql)
-    sums[3].begin()
-    sums[2].step()
-    sums[1].step()
-    to_tokens(1, kh, kl, True)
-    sums[3].step()
-    sums[0].step()
-    to_tokens(0, qh, ql, True)
     sums[1].step()
 
     vec_ref[...] = jnp.zeros_like(vec_ref)
@@ -519,7 +529,8 @@
         m2 = jnp.mean(dx * xhat, axis=-1, keepdims=True)
         g_ref[r, :] += rstd_ref[r, :] * (dx - m1 - xhat * m2)
 
-    halo_d = halo_back(g_ref, tile_t, 8)
+    halo_d = [halo_back(g_ref, tile_t, first, pl.ds(lane, part)) for first, lane in ((8, 0), (16, part))]
+    keep_own(g_ref, tile_t)
 
     sums[0].step()
     sums[1].step()
@@ -532,9 +543,10 @@
     sums[2].step()
     sums[3].step()
 
-    finish(halo_d)
+    finish(halo_d[0])
     sa1[...] = pick(table, tile_t[:, :part], NN)
     back0 = send_lat(sa1, ra1, lat_s.at[2], lat_r.at[2], a, b)
+    finish(halo_d[1])
     sa0[:, :part] = pick(table2, tile_t[:, part:], NN)
     back1 = send_lon(sa0, ra0, lon_s.at[2], lon_r.at[2], a, b, part)
     masked = jnp.where(cell_ref[...] >= 0, 1.0 - seen, 0.0)
@@ -557,12 +569,16 @@
         if k < 6:
             vec_begin(k + 1)
 
+    def round_of_sums():
+        for total in sums:
+            if total.stage < 8:
+                total.step()
+        if vec_copies and len(vec_copies) < 7:
+            vec_step()
+
     vec_begin(0)
-    sums[0].step()
-    sums[1].step()
-    sums[2].step()
-    sums[3].step()
-    vec_step()
+    round_of_sums()
+    round_of_sums()
 
     finish(back0)
     sa1[...] = pick(swap, ra1[...], NN)
@@ -571,11 +587,8 @@
     sa0[:, :part] = pick(swap, ra0[:, :part], TN)
     back1 = send_lat(sa0, rb0, lat_s.at[3], lat_r.at[3], a, b, part)
 
-    for _ in range(2):
-        for total in sums:
-            if total.stage < 8:
-                total.step()
-        vec_step()
+    for _ in range(4):
+        round_of_sums()
 
     finish(back0)
     finish(back1)
@@ -583,15 +596,8 @@
     denc_ref[:, :part] = pick(onehot(slots == column2), rb1[...], NN)
     denc_ref[:, part:] = pick(onehot(slots == column1), rb0[:, :part], NN)
 
-    while any(total.stage < 8 for total in sums):
-        front = min(total.stage for total in sums)
-        for total in sums:
-            if total.stage == front:
-                total.step()
-        if len(vec_copies) < 7:
-            vec_step()
-    while len(vec_copies) < 7:
-        vec_step()
+    while any(total.stage < 8 for total in sums) or len(vec_copies) < 7:
+        round_of_sums()
     vec_step()
     lanes = lax.broadcasted_iota(jnp.int32, (width, 128), 1)
     mine = jnp.logical_and(lax.broadcasted_iota(jnp.int32, (width, 128), 0) == b * 80 + lanes, lanes < 80)
@@ -626,7 +632,7 @@
         out_specs=[anyspace] + [vm] * 6,
         scratch_shapes=[
             v((2, 4, 4, 2, SHARD, inner), F32), v((width, 3 * inner), BF16), v((width, 3 * inner), BF16),
-            v((2, inner, part), BF16), v((2, inner, part), BF16), v((4, 4, 4, SHARD, inner), F32),
+            v((inner, width), BF16), v((inner, width), BF16), v((4, 4, 4, SHARD, inner), F32),
             v((4, 2, 2, 2, SHARD, inner), F32), v((4, 2, 2, SHARD, inner), F32),
             v((4, 2, SHARD, inner), F32), v((4, SHARD, inner), F32), v((4, 2, SHARD, inner), F32),
             v((4, 2, SHARD, inner), F32), v((7, 8, width), F32),
@@ -637,7 +643,7 @@
             v((rows, 1), F32), v((rows, width), BF16), v((rows, width), BF16),
             v((rows, 3 * inner), F32), v((2 * inner // HEAD, rows // 2, rows // 2), F32),
             v((rows, inner), F32), v((rows, inner), F32), v((rows, 3 * inner), F32),
-            v((8, width), F32), dma((6,)), dma((16,)), dma((16,)), dma((4, 15)), dma((4, 15)), dma((4, 7)), dma((4, 7)),
+            v((8, width), F32), dma((6,)), dma((20,)), dma((20,)), dma((4, 15)), dma((4, 15)), dma((4, 7)), dma((4, 7)),
             dma((4, 18)), dma((4, 18)), dma((7,)), dma((7,)), pltpu.SemaphoreType.REGULAR,
         ],
         compiler_params=pltpu.CompilerParams(
@@ -648,26 +654,20 @@
 
 
 def copy_kernel(*refs):
-    ins, outs, sems = refs[:6], refs[7:13], refs[15]
-    copies = [pltpu.make_async_copy(i, o, sems.at[k]) for k, (i, o) in enumerate(zip(ins, outs))]
-    for copy in copies:
-        copy.start()
+    for src, dst in zip(refs[:6], refs[7:13]):
+        dst[...] = src[...]
     refs[13][...] = refs[6][0:1, :80].reshape(80)
     refs[14][...] = refs[6][1:2, :80].reshape(80)
-    for copy in copies:
-        copy.wait()
 
 
 def hand_over(arrays, own):
     vm = pl.BlockSpec(memory_space=pltpu.VMEM)
-    anyspace = pl.BlockSpec(memory_space=pl.ANY)
     short = jax.ShapeDtypeStruct((80,), F32)
     return pl.pallas_call(
         copy_kernel,
         out_shape=tuple(jax.ShapeDtypeStruct(x.shape, x.dtype) for x in arrays) + (short, short),
-        in_specs=[anyspace] * 6 + [vm],
-        out_specs=[anyspace] * 6 + [vm] * 2,
-        scratch_shapes=[pltpu.SemaphoreType.DMA((6,))],
+        in_specs=[vm] * 7,
+        out_specs=[vm] * 8,
         compiler_params=pltpu.CompilerParams(vmem_limit_bytes=60 * 2**20),
         name="hand_over",
     )(*arrays, own)

time: 251 us -> 166 us (0.66)
  Pallas kernels: 249 us -> 165 us
    pallas_call x1, Pallas kernels: 83 us -> 3.27 us  [hand_over(): pl.pallas_call(copy_kernel, out_shape=tuple((jax.ShapeDtypeStruct(x.shape...]
    pallas_call x1, Pallas kernels: 166 us -> 162 us  [decoder_step(): pl.pallas_call(step_kernel, out_shape=(f((rows, width), F32), third, thir...]
where the time goes in v1:
time: 166 us
  Pallas kernels  165 us (99%)
    pallas_call x1, Pallas kernels, decoder_step(): pl.pallas_call(step_kernel, out_shape=(f((rows, width), F32), third, thir...  162 us

profile of v1, /device:TPU:0, one launch (start us, length us, event | category | flops | bytes accessed | tf_op | source)
XLA Modules:
  0.0 166.2 jit_solution(9254768191874111550)
XLA Ops:
  0.6 162.2 %decoder_step.1 = (f32[288,1280]{1,0:T(8,128)}, f32[2,40,640]{2,1,0:T(8,128)}, f32[2,40,640]{2,1,0:T(8,128)}, f32[2,40,640]{2,1,0:T(8,128)}, f32[40,1280]{1,0:T(...) custom-call(s32[1,304]{1,0:T(1,128)} %constant.6.cell_ref, s32[1,72]{1,0:T(1,128)} %bitcast.19, f32[72,1280]{1,0:T(8,128)} %enc_ref.1, ...), custom_call_target="tpu_custom_call" | custom-call | tf_op jit(solution)/shard_map/decoder_step/pallas_call | solution.py:625
  162.8 3.3 %hand_over.1 = (f32[288,1280]{1,0:T(8,128)}, f32[2,40,640]{2,1,0:T(8,128)}, f32[2,40,640]{2,1,0:T(8,128)}, f32[2,40,640]{2,1,0:T(8,128)}, f32[40,1280]{1,0:T(8,1...) custom-call(f32[288,1280]{1,0:T(8,128)} %get-tuple-element.23.refs_0_, f32[2,40,640]{2,1,0:T(8,128)} %get-tuple-element.24.refs_1_, ...), custom_call_target="tpu_custom_call" | custom-call | tf_op jit(solution)/shard_map/hand_over/pallas_call | solution.py:666

commit v2 on v1

--- a/solution.py
+++ b/solution.py
@@ -126,25 +126,25 @@
 
 
 class Sum:
-    def __init__(self, m, home, place, w, acc, r1, r2, r3, r4, r5, fin, send_sem, recv_sem):
-        self.m, self.home, self.place = m, home, place
-        self.w, self.acc, self.r = w, acc, (r1, r2, r3, r4, r5)
+    def __init__(self, m, place, acc, r1, r2, r3, r4, r5, fin, send_sem, recv_sem):
+        self.m, self.place = m, place
+        self.acc, self.r = acc, (r1, r2, r3, r4, r5)
         self.fin, self.send_sem, self.recv_sem = fin, send_sem, recv_sem
-        self.first = m % 2 == 0
-        self.stage, self.slot, self.copies = 0, 0, []
+        self.stage, self.slot, self.copies = 1, 0, []
+        a, b, x, c, y, z = place
+        self.me1, self.me2 = y * (1 - c) + z * c, z * (1 - c) + y * c
 
     def chunk(self, i, half):
-        rest = pl.ds(2 * half, 2)
-        return (self.m, i, rest) if self.first else (self.m, rest, i)
+        return (self.m, i, pl.ds(2 * half, 2))
 
     def piece(self, i, half):
+        return (self.m, self.me1, i, pl.ds(half * SHARD, SHARD))
+
+    def near(self, first, i):
         a, b, x, c, y, z = self.place
-        rows = pl.ds(0, 24) if half == 0 else pl.ds(24, 16)
-        return (self.m, y, i, rows) if self.first else (self.m, i, z, rows)
-
-    def near(self, ring, i):
-        a, b, x, c, y, z = self.place
-        return (a, i * 4 + z) if ring == self.first else (a, y * 4 + i)
+        along_y, along_z = i * 4 + z, y * 4 + i
+        core = c if first else 1 - c
+        return (a, along_y * (1 - core) + along_z * core)
 
     def send(self, src, dst, device):
         k = self.slot
@@ -154,17 +154,13 @@
     def begin(self):
         a, b, x, c, y, z = self.place
         m, acc, (r1, r2, r3, r4, r5) = self.m, self.acc, self.r
-        me1, me2 = (y, z) if self.first else (z, y)
-        s = self.stage
-        if s == 0:
-            self.send(self.w.at[self.home, :, :, 1 - c], acc.at[m], (a + 1 - 2 * c, b))
-            return
+        me1, me2, s = self.me1, self.me2, self.stage
         if s == 7:
             self.send(self.fin.at[m, c], self.fin.at[m, c], (a + 1 - 2 * c, b))
             return
         for half in range(2):
             q1, q2 = (flip_low, flip_far) if half == 0 else (flip_far, flip_low)
-            rows = pl.ds(0, 24) if half == 0 else pl.ds(24, 16)
+            rows = pl.ds(half * SHARD, SHARD)
             if s == 1:
                 p = q1(me1)
                 self.send(acc.at[self.chunk(p, half)], r1.at[m, 0, half], self.near(True, p))
@@ -187,17 +183,12 @@
     def end(self):
         a, b, x, c, y, z = self.place
         m, acc, (r1, r2, r3, r4, r5) = self.m, self.acc, self.r
-        me1, me2 = (y, z) if self.first else (z, y)
-        s = self.stage
+        me1, me2, s = self.me1, self.me2, self.stage
         finish(self.copies)
         self.copies = []
-        if s == 0:
-            @pl.loop(0, 4)
-            def _(i):
-                acc[m, i] += self.w[self.home, i, :, c]
         for half in range(2):
             q2 = flip_far if half == 0 else flip_low
-            rows = pl.ds(0, 24) if half == 0 else pl.ds(24, 16)
+            rows = pl.ds(half * SHARD, SHARD)
             if s == 1:
                 acc[self.chunk(me1, half)] += r1[m, 0, half]
                 acc[self.chunk(q2(me1), half)] += r1[m, 1, half]
@@ -222,11 +213,11 @@
 
 def step_kernel(
     cell_ref, pos_ref, enc_ref, mask_ref, gain_ref, cot_hbm, wq_hbm, wk_hbm, wv_hbm, wo_hbm,
-    decoded_hbm, dq_ref, dk_ref, dv_ref, do_ref, denc_ref, own_ref,
-    w, w_hi, w_lo, o_hi, o_lo, acc, r1, r2, r3, r4, r5, fin, vr,
+    decoded_hbm, dq_hbm, dk_hbm, dv_hbm, do_hbm, denc_hbm, own_ref,
+    w_hi, w_lo, o_hi, o_lo, acc, r1, r2, r3, r4, r5, fin, vr,
     tile_t, tile_g, land_t, land_g, sa0, ra0, rb0, sa1, ra1, rb1,
-    t_ref, g_ref, xhat_ref, dn_ref, rstd_ref, n_hi, n_lo, qkv_ref, p_ref, att_ref, datt_ref, dqkv_ref,
-    vec_ref, load_s, halo_s, halo_r, lon_s, lon_r, lat_s, lat_r, sum_s, sum_r, vec_s, vec_r, free_s,
+    t_ref, g_ref, xhat_ref, rstd_ref, n_hi, n_lo, qkv_ref, p_ref, att_ref, datt_ref, dqkv_ref,
+    vec_ref, px_ref, pg_ref, pa_ref, pd_ref, pair_s, pair_r, load_s, halo_s, halo_r, lon_s, lon_r, lat_s, lat_r, sum_s, sum_r, vec_s, vec_r, free_s,
 ):
     a, b = lax.axis_index("lat"), lax.axis_index("lon")
     x, c = a // 2, a % 2
@@ -241,12 +232,12 @@
 
     load_cot = pltpu.make_async_copy(cot_hbm, xhat_ref, load_s.at[0])
     load_o = [
-        pltpu.make_async_copy(wo_hbm.at[:, :, :, pl.ds(i * part, part)], w.at[0, :, :, i], load_s.at[1 + i])
+        pltpu.make_async_copy(wo_hbm.at[:, :, :, pl.ds(i * part, part)], acc.at[0, :, :, pl.ds(i * SHARD, SHARD)], load_s.at[1 + i])
         for i in range(2)
     ]
-    load_v = pltpu.make_async_copy(wv_hbm, w.at[1], load_s.at[3])
-    load_k = pltpu.make_async_copy(wk_hbm, w.at[0], load_s.at[4])
-    load_q = pltpu.make_async_copy(wq_hbm, w.at[1], load_s.at[5])
+    load_v = pltpu.make_async_copy(wv_hbm, acc.at[1], load_s.at[3])
+    load_k = pltpu.make_async_copy(wk_hbm, acc.at[0], load_s.at[4])
+    load_q = pltpu.make_async_copy(wq_hbm, acc.at[1], load_s.at[5])
     load_cot.start()
     load_o[0].start()
     load_o[1].start()
@@ -259,7 +250,7 @@
         def _(i):
             r = pl.ds(pl.multiple_of(i * 80, 80), 80)
             cols = slice(which * inner, (which + 1) * inner)
-            w_hi[r, cols], w_lo[r, cols] = split(w[home, i // 4, i % 4].reshape(80, inner))
+            w_hi[r, cols], w_lo[r, cols] = split(acc[home, i // 4, i % 4])
 
     peers = [(a, (b + k) % 16) for k in range(1, 16)] + [((a + k) % 8, b) for k in range(1, 8)]
     peers += [(up, right), (down, left)]
@@ -342,7 +333,7 @@
         for j in range(4):
             r = slice(j * 160, (j + 1) * 160)
             cols = slice(i * part, (i + 1) * part)
-            o_hi[r, cols], o_lo[r, cols] = split(w[0, j, :, i].reshape(160, part))
+            o_hi[r, cols], o_lo[r, cols] = split(acc[0, j, :, i * SHARD:(i + 1) * SHARD].reshape(160, part))
     load_k.start()
     take_weight(load_v, 1, 2)
     load_q.start()
@@ -392,6 +383,13 @@
         cols = pl.ds(pl.multiple_of(j * 256, 256), 256)
         qkv_ref[:, cols] = dot3((n_hi[...], n_lo[...]), (w_hi[:, cols], w_lo[:, cols]), NN)
 
+    partner = (a + 1 - 2 * c, b)
+
+    def give(src, dst, k):
+        return remote(src, dst, pair_s.at[k], pair_r.at[k], partner)
+
+    gifts = [give(xhat_ref, px_ref, 0)]
+
     qkv_ref[:, 1792:] = dot3((n_hi[...], n_lo[...]), (w_hi[:, 1792:], w_lo[:, 1792:]), NN)
 
     finish(halo_g)
@@ -400,6 +398,7 @@
     for peer in peers:
         pl.semaphore_signal(free_s, inc=1, device_id=peer, device_id_type=MESH)
 
+    gifts.append(give(g_ref, pg_ref, 1))
     datt_ref[...] = dot3(split(g_ref[...]), (o_hi[...], o_lo[...]), NT)
 
     att_ref[...] = jnp.zeros_like(att_ref)
@@ -433,6 +432,11 @@
             att_ref[r, lo:hi] += jnp.where(mine, dot3(p, v, NN), 0.0)
             dqkv_ref[r, 2 * inner + lo:2 * inner + hi] += dot3(p, do, TN)
 
+    sa0[:, :inner] = jnp.where(c == 0, dqkv_ref[:SLOTS, 2 * inner:], att_ref[:SLOTS, :])
+    sa1[:rows - SLOTS, :] = jnp.where(c == 0, dqkv_ref[SLOTS:, 2 * inner:], att_ref[SLOTS:, :])
+    gifts.append(give(sa0.at[:, pl.ds(0, inner)], pa_ref.at[pl.ds(0, SLOTS)], 2))
+    gifts.append(give(sa1.at[pl.ds(0, rows - SLOTS)], pa_ref.at[pl.ds(SLOTS, rows - SLOTS)], 4))
+
     att = split(att_ref[...])
     att_row = jnp.concatenate([att[0], att[0], att[1]], axis=1)
 
@@ -446,15 +450,36 @@
     halo_o = halo_back(t_ref, tile_g, 12, pl.ds(0, width))
     keep_own(t_ref, tile_g)
 
-    sums = [
-        Sum(m, m % 2, (a, b, x, c, y, z), w, acc, r1, r2, r3, r4, r5, fin, sum_s, sum_r) for m in range(4)
-    ]
-
-    att3 = jnp.concatenate([att[0], att[0], att[1]], axis=0)
-    gh, gl = split(g_ref[...])
-    res = dot(att3, jnp.concatenate([gh, gl, gh], axis=0), TN)
-    for i in range(2):
-        w[0, :, :, i] = res[:, i * part:(i + 1) * part].reshape(4, 4, SHARD, part)
+    sums = [Sum(m, (a, b, x, c, y, z), acc, r1, r2, r3, r4, r5, fin, sum_s, sum_r) for m in range(2)]
+
+    def left_rows(own, other):
+        return jnp.concatenate([own[0], own[0], own[1], other[0], other[0], other[1]], axis=0)
+
+    def right_rows(own, other):
+        return jnp.concatenate([own[0], own[1], own[0], other[0], other[1], other[0]], axis=0)
+
+    def normed_rows(i):
+        cols = slice(i * part, (i + 1) * part)
+        return left_rows((n_hi[:, cols], n_lo[:, cols]), split(px_ref[:, cols] * gain[:, cols]))
+
+    finish(gifts)
+
+    @pl.when(c == 0)
+    def _():
+        left6 = left_rows(split(att_ref[...]), split(pa_ref[...]))
+        for i in range(2):
+            cols = slice(i * part, (i + 1) * part)
+            right6 = right_rows(split(g_ref[:, cols]), split(pg_ref[:, cols]))
+            acc[0, :, :, i * SHARD:(i + 1) * SHARD] = dot(left6, right6, TN).reshape(4, 4, SHARD, part)
+
+    @pl.when(c == 1)
+    def _():
+        right6 = right_rows(split(dqkv_ref[:, 2 * inner:]), split(pa_ref[...]))
+        for i in range(2):
+            res = dot(normed_rows(i), right6, TN).reshape(2, 4, 2 * SHARD, inner)
+            for j in range(2):
+                acc[0, :, 2 * i + j] = res[j]
+
     sums[0].begin()
 
     def grad_rows(which):
@@ -467,25 +492,10 @@
             r = slice(lo, lo + 256)
             wh, wl = w_hi[r, cols], w_lo[r, cols]
             res = dot(d3, jnp.concatenate([wh, wl, wh], axis=1), NT)
-            dn_ref[:, r] = dn_ref[:, r] + res if add else res
-
-    def to_weight(cols, homes):
-        dh, dl = split(dqkv_ref[:, cols])
-        d3 = jnp.concatenate([dh, dl, dh], axis=0)
-        for i in range(2):
-            half = slice(i * part, (i + 1) * part)
-            nh, nl = n_hi[:, half], n_lo[:, half]
-            res = dot(jnp.concatenate([nh, nh, nl], axis=0), d3, TN)
-            for j, home in enumerate(homes):
-                block = res[:, j * inner:(j + 1) * inner]
-                w[home, 2 * i:2 * i + 2] = block.reshape(2, 4, 2, SHARD, inner)
-
-    to_weight(slice(2 * inner, 3 * inner), (1,))
-    sums[1].begin()
-    sums[0].step()
+            pg_ref[:, r] = pg_ref[:, r] + res if add else res
+
     dh, dl = grad_rows(2)
     to_tokens(2, dh, dl, False)
-    sums[1].step()
 
     @pl.loop(0, 2)
     def _(wd):
@@ -502,26 +512,23 @@
             dqkv_ref[r, lo:hi] += jnp.where(mine, dot3(ds, k, NN) * norm, 0.0)
             dqkv_ref[r, inner + lo:inner + hi] += dot3(ds, q, TN)
 
-    to_weight(slice(0, 2 * inner), (1, 0))
-    sums[2].begin()
-    sums[3].begin()
+    def lanes_of(core):
+        return pl.ds(pl.multiple_of(core * inner, 128), inner)
+
+    gift = give(dqkv_ref.at[:, lanes_of(1 - c)], pd_ref, 3)
     sums[0].step()
-    sums[1].step()
     kh, kl = grad_rows(1)
     to_tokens(1, kh, kl, True)
-    sums[2].step()
-    sums[3].step()
     qh, ql = grad_rows(0)
     to_tokens(0, qh, ql, True)
     sums[0].step()
-    sums[1].step()
 
     vec_ref[...] = jnp.zeros_like(vec_ref)
 
     @pl.loop(0, rows // step)
     def _(i):
         r = pl.ds(pl.multiple_of(i * step, step), step)
-        dn = dn_ref[r, :]
+        dn = pg_ref[r, :]
         xhat = xhat_ref[r, :]
         vec_ref[1:2, :] += jnp.sum(dn * xhat, axis=0, keepdims=True)
         dx = dn * gain
@@ -532,16 +539,23 @@
     halo_d = [halo_back(g_ref, tile_t, first, pl.ds(lane, part)) for first, lane in ((8, 0), (16, part))]
     keep_own(g_ref, tile_t)
 
+    gift.wait()
+    right6 = right_rows(split(dqkv_ref[:, lanes_of(c)]), split(pd_ref[...]))
+    for i in range(2):
+        res = dot(normed_rows(i), right6, TN).reshape(2, 4, 2 * SHARD, inner)
+        for j in range(2):
+            for k in range(4):
+                at_y, at_z = 2 * i + j, k
+                acc[1, at_y * (1 - c) + at_z * c, at_z * (1 - c) + at_y * c] = res[j, k]
+    sums[1].begin()
     sums[0].step()
-    sums[1].step()
 
     finish(halo_o)
     for j in range(0, width, 256):
         xhat_ref[:, j:j + 256] = pick(place, tile_g[:, j:j + 256], NN)
     store = pltpu.make_async_copy(xhat_ref, decoded_hbm, load_s.at[0])
     store.start()
-    sums[2].step()
-    sums[3].step()
+    sums[0].step()
 
     finish(halo_d[0])
     sa1[...] = pick(table, tile_t[:, :part], NN)
@@ -578,7 +592,6 @@
 
     vec_begin(0)
     round_of_sums()
-    round_of_sums()
 
     finish(back0)
     sa1[...] = pick(swap, ra1[...], NN)
@@ -587,14 +600,16 @@
     sa0[:, :part] = pick(swap, ra0[:, :part], TN)
     back1 = send_lat(sa0, rb0, lat_s.at[3], lat_r.at[3], a, b, part)
 
-    for _ in range(4):
+    for _ in range(5):
         round_of_sums()
 
     finish(back0)
     finish(back1)
     slots = lax.broadcasted_iota(jnp.int32, (count, SLOTS), 1).astype(F32)
-    denc_ref[:, :part] = pick(onehot(slots == column2), rb1[...], NN)
-    denc_ref[:, part:] = pick(onehot(slots == column1), rb0[:, :part], NN)
+    tile_g[:count, :part] = pick(onehot(slots == column2), rb1[...], NN)
+    tile_g[:count, part:] = pick(onehot(slots == column1), rb0[:, :part], NN)
+    store_enc = pltpu.make_async_copy(tile_g.at[pl.ds(0, count)], denc_hbm, load_s.at[6])
+    store_enc.start()
 
     while any(total.stage < 8 for total in sums) or len(vec_copies) < 7:
         round_of_sums()
@@ -604,12 +619,19 @@
     mine = onehot(mine)
     hi, mid, lo = split3(vec_ref[...] * SCALE)
     own_ref[...] = (dot(hi, mine, NN) + dot(mid, mine, NN)) + dot(lo, mine, NN)
-    do_ref[:, :part] = fin[0, 0]
-    do_ref[:, part:] = fin[0, 1]
-    dv_ref[...] = fin[1]
-    dk_ref[...] = fin[2]
-    dq_ref[...] = fin[3]
+    stores = [
+        pltpu.make_async_copy(fin.at[0, 0, pl.ds(0, SHARD)], do_hbm.at[:, pl.ds(0, part)], load_s.at[1]),
+        pltpu.make_async_copy(fin.at[0, 0, pl.ds(SHARD, SHARD)], do_hbm.at[:, pl.ds(part, part)], load_s.at[2]),
+        pltpu.make_async_copy(fin.at[0, 1], dv_hbm, load_s.at[3]),
+        pltpu.make_async_copy(fin.at[1, 0], dq_hbm, load_s.at[4]),
+        pltpu.make_async_copy(fin.at[1, 1], dk_hbm, load_s.at[5]),
+    ]
+    for copy in stores:
+        copy.start()
     store.wait()
+    store_enc.wait()
+    for copy in stores:
+        copy.wait()
 
 
 def decoder_step(cell, pos, enc, mask, gain, cot, wq, wk, wv, wo):
@@ -621,7 +643,7 @@
     f = jax.ShapeDtypeStruct
     dma = pltpu.SemaphoreType.DMA
     v = pltpu.VMEM
-    third = f((2, SHARD, inner), F32)
+    third = f((2 * SHARD, inner), F32)
     return pl.pallas_call(
         step_kernel,
         out_shape=(
@@ -629,22 +651,23 @@
             f((8, 128), F32),
         ),
         in_specs=[vm] * 5 + [anyspace] * 5,
-        out_specs=[anyspace] + [vm] * 6,
+        out_specs=[anyspace] * 6 + [vm],
         scratch_shapes=[
-            v((2, 4, 4, 2, SHARD, inner), F32), v((width, 3 * inner), BF16), v((width, 3 * inner), BF16),
-            v((inner, width), BF16), v((inner, width), BF16), v((4, 4, 4, SHARD, inner), F32),
-            v((4, 2, 2, 2, SHARD, inner), F32), v((4, 2, 2, SHARD, inner), F32),
-            v((4, 2, SHARD, inner), F32), v((4, SHARD, inner), F32), v((4, 2, SHARD, inner), F32),
-            v((4, 2, SHARD, inner), F32), v((7, 8, width), F32),
+            v((width, 3 * inner), BF16), v((width, 3 * inner), BF16),
+            v((inner, width), BF16), v((inner, width), BF16), v((2, 4, 4, 2 * SHARD, inner), F32),
+            v((2, 2, 2, 2, 2 * SHARD, inner), F32), v((2, 2, 2, 2 * SHARD, inner), F32),
+            v((2, 2, 2 * SHARD, inner), F32), v((2, 2 * SHARD, inner), F32), v((2, 2, 2 * SHARD, inner), F32),
+            v((2, 2, 2 * SHARD, inner), F32), v((7, 8, width), F32),
             v((TROWS, width), F32), v((TROWS, width), F32), v((120, width), F32), v((120, width), F32),
             v((SLOTS, part + 128), F32), v((SLOTS, part + 128), F32), v((SLOTS, part + 128), F32),
             v((SLOTS, part), F32), v((SLOTS, part), F32), v((SLOTS, part), F32),
-            v((rows, width), F32), v((rows, width), F32), v((rows, width), F32), v((rows, width), F32),
+            v((rows, width), F32), v((rows, width), F32), v((rows, width), F32),
             v((rows, 1), F32), v((rows, width), BF16), v((rows, width), BF16),
             v((rows, 3 * inner), F32), v((2 * inner // HEAD, rows // 2, rows // 2), F32),
             v((rows, inner), F32), v((rows, inner), F32), v((rows, 3 * inner), F32),
-            v((8, width), F32), dma((6,)), dma((20,)), dma((20,)), dma((4, 15)), dma((4, 15)), dma((4, 7)), dma((4, 7)),
-            dma((4, 18)), dma((4, 18)), dma((7,)), dma((7,)), pltpu.SemaphoreType.REGULAR,
+            v((8, width), F32), v((rows, width), F32), v((rows, width), F32), v((rows, inner), F32), v((rows, inner), F32),
+            dma((5,)), dma((5,)), dma((7,)), dma((20,)), dma((20,)), dma((4, 15)), dma((4, 15)), dma((4, 7)), dma((4, 7)),
+            dma((2, 17)), dma((2, 17)), dma((7,)), dma((7,)), pltpu.SemaphoreType.REGULAR,
         ],
         compiler_params=pltpu.CompilerParams(
             vmem_limit_bytes=63 * 2**20, collective_id=0, has_side_effects=True
@@ -676,7 +699,7 @@
 def body(positions, encoded, mask_token, norm_gain, w_query, w_key, w_value, w_out, cotangent):
     model_width = encoded.shape[1]
     inner = w_out.shape[0]
-    shard = (4, 4, 2, SHARD, inner)
+    shard = (4, 4, 2 * SHARD, inner)
     tile_map = jnp.asarray(tile_rows_map())[None]
     *arrays, own = decoder_step(
         tile_map, positions[None], encoded, mask_token.reshape(-1, 128), norm_gain.reshape(-1, 128),
@@ -684,8 +707,7 @@
         w_value.reshape(shard), w_out.reshape(4, 4, SHARD, model_width),
     )
     decoded, grad_query, grad_key, grad_value, grad_out, grad_encoded, grad_mask, grad_gain = hand_over(arrays, own)
-    matrices = (g.reshape(-1, inner) for g in (grad_query, grad_key, grad_value))
-    return (decoded.reshape(cotangent.shape), *matrices, grad_out, grad_mask, grad_gain, grad_encoded)
+    return (decoded.reshape(cotangent.shape), grad_query, grad_key, grad_value, grad_out, grad_mask, grad_gain, grad_encoded)
 
 
 def solution(mesh):

time: 166 us -> 171 us (1.030)
  Pallas kernels: 165 us -> 170 us
    pallas_call x1, Pallas kernels: 162 us -> 167 us  [decoder_step(): pl.pallas_call(step_kernel, out_shape=(f((rows, width), F32), third, thir...]
where the time goes in v2:
time: 171 us
  Pallas kernels  170 us (99%)
    pallas_call x1, Pallas kernels, decoder_step(): pl.pallas_call(step_kernel, out_shape=(f((rows, width), F32), third, thir...  167 us

profile of v2, /device:TPU:0, one launch (start us, length us, event | category | flops | bytes accessed | tf_op | source)
XLA Modules:
  0.0 170.8 jit_solution(6513882695054176677)
XLA Ops:
  0.6 166.8 %decoder_step.1 = (f32[288,1280]{1,0:T(8,128)}, f32[80,640]{1,0:T(8,128)}, f32[80,640]{1,0:T(8,128)}, f32[80,640]{1,0:T(8,128)}, f32[40,1280]{1,0:T(8,128)}, /*index=5*/f32[72,1280]{1,0:T(8,128)}, f32[8,128]{1,0:T(8,128)}) custom-call(s32[1,304]{1,0:T(1,128)} %constant.6.cell_ref, s32[1,72]{1,0:T(1,128)} %bitcast.16, f32[72,1280]{1,0:T(8,128)} %enc_ref.1, ...), custom_call_target="tpu_custom_call" | custom-call | tf_op jit(solution)/shard_map/decoder_step/pallas_call | solution.py:647
  167.4 3.3 %hand_over.1 = (f32[288,1280]{1,0:T(8,128)}, f32[80,640]{1,0:T(8,128)}, f32[80,640]{1,0:T(8,128)}, f32[80,640]{1,0:T(8,128)}, f32[40,1280]{1,0:T(8,128)}, /*inde...) custom-call(f32[288,1280]{1,0:T(8,128)} %get-tuple-element.23.refs_0_, f32[80,640]{1,0:T(8,128)} %get-tuple-element.24.refs_1_, ...), custom_call_target="tpu_custom_call" | custom-call | tf_op jit(solution)/shard_map/hand_over/pallas_call | solution.py:689

commit v3 on v1

--- a/solution.py
+++ b/solution.py
@@ -26,7 +26,11 @@
 
 
 def dot3(a, b, dims):
-    return dot(a[0], b[0], dims) + (dot(a[0], b[1], dims) + dot(a[1], b[0], dims))
+    if dims == TN:
+        return dot(a[0], b[0], dims) + (dot(a[0], b[1], dims) + dot(a[1], b[0], dims))
+    rows = a[0].shape[0]
+    both = dot(jnp.concatenate([a[0], a[1]], axis=0), b[0], dims)
+    return both[:rows] + (both[rows:] + dot(a[0], b[1], dims))
 
 
 def head_lanes(h):
@@ -52,16 +56,9 @@
     return np.array(order, np.int32)
 
 
-def split3(x):
-    hi = x.astype(BF16)
-    rest = x - hi.astype(F32)
-    mid = rest.astype(BF16)
-    return hi, mid, (rest - mid.astype(F32)).astype(BF16)
-
-
 def pick(onehot, x, dims):
-    hi, mid, lo = split3(x)
-    return (dot(onehot, hi, dims) + dot(onehot, mid, dims)) + dot(onehot, lo, dims)
+    hi, lo = split(x)
+    return dot(onehot, hi, dims) + dot(onehot, lo, dims)
 
 
 def onehot(cond):
@@ -602,8 +599,8 @@
     lanes = lax.broadcasted_iota(jnp.int32, (width, 128), 1)
     mine = jnp.logical_and(lax.broadcasted_iota(jnp.int32, (width, 128), 0) == b * 80 + lanes, lanes < 80)
     mine = onehot(mine)
-    hi, mid, lo = split3(vec_ref[...] * SCALE)
-    own_ref[...] = (dot(hi, mine, NN) + dot(mid, mine, NN)) + dot(lo, mine, NN)
+    hi, lo = split(vec_ref[...] * SCALE)
+    own_ref[...] = dot(hi, mine, NN) + dot(lo, mine, NN)
     do_ref[:, :part] = fin[0, 0]
     do_ref[:, part:] = fin[0, 1]
     dv_ref[...] = fin[1]
@@ -654,20 +651,30 @@
 
 
 def copy_kernel(*refs):
-    for src, dst in zip(refs[:6], refs[7:13]):
-        dst[...] = src[...]
+    ins, outs, kept, sems = refs[:6], refs[7:13], refs[15:21], refs[21]
+    loads = [pltpu.make_async_copy(src, via, sems.at[0, k]) for k, (src, via) in enumerate(zip(ins, kept))]
+    stores = [pltpu.make_async_copy(via, dst, sems.at[1, k]) for k, (via, dst) in enumerate(zip(kept, outs))]
+    for load in loads:
+        load.start()
     refs[13][...] = refs[6][0:1, :80].reshape(80)
     refs[14][...] = refs[6][1:2, :80].reshape(80)
+    for load, store in zip(loads[::-1], stores[::-1]):
+        load.wait()
+        store.start()
+    for store in stores:
+        store.wait()
 
 
 def hand_over(arrays, own):
     vm = pl.BlockSpec(memory_space=pltpu.VMEM)
+    anyspace = pl.BlockSpec(memory_space=pl.ANY)
     short = jax.ShapeDtypeStruct((80,), F32)
     return pl.pallas_call(
         copy_kernel,
         out_shape=tuple(jax.ShapeDtypeStruct(x.shape, x.dtype) for x in arrays) + (short, short),
-        in_specs=[vm] * 7,
-        out_specs=[vm] * 8,
+        in_specs=[anyspace] * 6 + [vm],
+        out_specs=[anyspace] * 6 + [vm] * 2,
+        scratch_shapes=[pltpu.VMEM(x.shape, x.dtype) for x in arrays] + [pltpu.SemaphoreType.DMA((2, 6))],
         compiler_params=pltpu.CompilerParams(vmem_limit_bytes=60 * 2**20),
         name="hand_over",
     )(*arrays, own)

time: 166 us -> 167 us (level)
  no operation moved by 1% of the time
where the time goes in v3:
time: 167 us
  Pallas kernels  166 us (99%)
    pallas_call x1, Pallas kernels, decoder_step(): pl.pallas_call(step_kernel, out_shape=(f((rows, width), F32), third, thir...  161 us
    pallas_call x1, Pallas kernels, hand_over(): pl.pallas_call(copy_kernel, out_shape=tuple((jax.ShapeDtypeStruct(x.shape...  4.48 us

profile of v3, /device:TPU:0, one launch (start us, length us, event | category | flops | bytes accessed | tf_op | source)
XLA Modules:
  0.0 166.7 jit_solution(1129976549666089251)
XLA Ops:
  0.6 161.4 %decoder_step.1 = (f32[288,1280]{1,0:T(8,128)}, f32[2,40,640]{2,1,0:T(8,128)}, f32[2,40,640]{2,1,0:T(8,128)}, f32[2,40,640]{2,1,0:T(8,128)}, f32[40,1280]{1,0:T(...) custom-call(s32[1,304]{1,0:T(1,128)} %constant.6.cell_ref, s32[1,72]{1,0:T(1,128)} %bitcast.19, f32[72,1280]{1,0:T(8,128)} %enc_ref.1, ...), custom_call_target="tpu_custom_call" | custom-call | tf_op jit(solution)/shard_map/decoder_step/pallas_call | solution.py:622
  162.0 4.5 %hand_over.1 = (f32[288,1280]{1,0:T(8,128)}, f32[2,40,640]{2,1,0:T(8,128)}, f32[2,40,640]{2,1,0:T(8,128)}, f32[2,40,640]{2,1,0:T(8,128)}, f32[40,1280]{1,0:T(8,1...) custom-call(f32[288,1280]{1,0:T(8,128)} %get-tuple-element.23.refs_0_, f32[2,40,640]{2,1,0:T(8,128)} %get-tuple-element.24.refs_1_, ...), custom_call_target="tpu_custom_call" | custom-call | tf_op jit(solution)/shard_map/hand_over/pallas_call | solution.py:672

commit v4 on v3

--- a/solution.py
+++ b/solution.py
@@ -391,14 +391,6 @@
 
     qkv_ref[:, 1792:] = dot3((n_hi[...], n_lo[...]), (w_hi[:, 1792:], w_lo[:, 1792:]), NN)
 
-    finish(halo_g)
-    settle(tile_g, land_g, g_ref)
-
-    for peer in peers:
-        pl.semaphore_signal(free_s, inc=1, device_id=peer, device_id_type=MESH)
-
-    datt_ref[...] = dot3(split(g_ref[...]), (o_hi[...], o_lo[...]), NT)
-
     att_ref[...] = jnp.zeros_like(att_ref)
     dqkv_ref[...] = jnp.zeros_like(dqkv_ref)
     is_last = a == 7
@@ -420,7 +412,6 @@
             q = split(jnp.where(mine, qkv_ref[r, lo:hi] * norm, 0.0))
             k = split(qkv_ref[r, inner + lo:inner + hi])
             v = split(qkv_ref[r, 2 * inner + lo:2 * inner + hi])
-            do = split(jnp.where(mine, datt_ref[r, lo:hi], 0.0))
             s = dot3(q, k, NT)
             s = jnp.where(blocked, -1e30, s)
             e = jnp.exp(s - jnp.max(s, axis=-1, keepdims=True))
@@ -428,31 +419,26 @@
             p_ref[wd * heads + h] = p32
             p = split(p32)
             att_ref[r, lo:hi] += jnp.where(mine, dot3(p, v, NN), 0.0)
-            dqkv_ref[r, 2 * inner + lo:2 * inner + hi] += dot3(p, do, TN)
-
-    att = split(att_ref[...])
-    att_row = jnp.concatenate([att[0], att[0], att[1]], axis=1)
-
-    @pl.loop(0, width // 256)
-    def _(j):
-        cols = pl.ds(pl.multiple_of(j * 256, 256), 256)
-        oh, ol = o_hi[:, cols], o_lo[:, cols]
-        t_ref[:, cols] += dot(att_row, jnp.concatenate([oh, ol, oh], axis=0), NN)
-
-    pl.semaphore_wait(free_s, len(peers))
-    halo_o = halo_back(t_ref, tile_g, 12, pl.ds(0, width))
-    keep_own(t_ref, tile_g)
+
+    finish(halo_g)
+    settle(tile_g, land_g, g_ref)
+
+    for peer in peers:
+        pl.semaphore_signal(free_s, inc=1, device_id=peer, device_id_type=MESH)
+
+    datt_ref[...] = dot3(split(g_ref[...]), (o_hi[...], o_lo[...]), NT)
+
+    @pl.loop(0, 2)
+    def _(wd):
+        r = pl.ds(pl.multiple_of(wd * half, 16), half)
+        for h in range(heads):
+            lo, hi, mine = head(h)
+            do = split(jnp.where(mine, datt_ref[r, lo:hi], 0.0))
+            dqkv_ref[r, 2 * inner + lo:2 * inner + hi] += dot3(split(p_ref[wd * heads + h]), do, TN)
 
     sums = [
         Sum(m, m % 2, (a, b, x, c, y, z), w, acc, r1, r2, r3, r4, r5, fin, sum_s, sum_r) for m in range(4)
     ]
-
-    att3 = jnp.concatenate([att[0], att[0], att[1]], axis=0)
-    gh, gl = split(g_ref[...])
-    res = dot(att3, jnp.concatenate([gh, gl, gh], axis=0), TN)
-    for i in range(2):
-        w[0, :, :, i] = res[:, i * part:(i + 1) * part].reshape(4, 4, SHARD, part)
-    sums[0].begin()
 
     def grad_rows(which):
         return split(dqkv_ref[:, which * inner:(which + 1) * inner])
@@ -479,10 +465,30 @@
 
     to_weight(slice(2 * inner, 3 * inner), (1,))
     sums[1].begin()
-    sums[0].step()
+    att = split(att_ref[...])
+    att3 = jnp.concatenate([att[0], att[0], att[1]], axis=0)
+    gh, gl = split(g_ref[...])
+    res = dot(att3, jnp.concatenate([gh, gl, gh], axis=0), TN)
+    for i in range(2):
+        w[0, :, :, i] = res[:, i * part:(i + 1) * part].reshape(4, 4, SHARD, part)
+    sums[0].begin()
+
+    att_row = jnp.concatenate([att[0], att[0], att[1]], axis=1)
+
+    @pl.loop(0, width // 256)
+    def _(j):
+        cols = pl.ds(pl.multiple_of(j * 256, 256), 256)
+        oh, ol = o_hi[:, cols], o_lo[:, cols]
+        t_ref[:, cols] += dot(att_row, jnp.concatenate([oh, ol, oh], axis=0), NN)
+
+    pl.semaphore_wait(free_s, len(peers))
+    halo_o = halo_back(t_ref, tile_g, 12, pl.ds(0, width))
+    keep_own(t_ref, tile_g)
+
     dh, dl = grad_rows(2)
     to_tokens(2, dh, dl, False)
     sums[1].step()
+    sums[0].step()
 
     @pl.loop(0, 2)
     def _(wd):
@@ -506,8 +512,6 @@
     sums[1].step()
     kh, kl = grad_rows(1)
     to_tokens(1, kh, kl, True)
-    sums[2].step()
-    sums[3].step()
     qh, ql = grad_rows(0)
     to_tokens(0, qh, ql, True)
     sums[0].step()
@@ -527,6 +531,8 @@
         g_ref[r, :] += rstd_ref[r, :] * (dx - m1 - xhat * m2)
 
     halo_d = [halo_back(g_ref, tile_t, first, pl.ds(lane, part)) for first, lane in ((8, 0), (16, part))]
+    sums[2].step()
+    sums[3].step()
     keep_own(g_ref, tile_t)
 
     sums[0].step()
@@ -537,8 +543,6 @@
         xhat_ref[:, j:j + 256] = pick(place, tile_g[:, j:j + 256], NN)
     store = pltpu.make_async_copy(xhat_ref, decoded_hbm, load_s.at[0])
     store.start()
-    sums[2].step()
-    sums[3].step()
 
     finish(halo_d[0])
     sa1[...] = pick(table, tile_t[:, :part], NN)
@@ -651,30 +655,20 @@
 
 
 def copy_kernel(*refs):
-    ins, outs, kept, sems = refs[:6], refs[7:13], refs[15:21], refs[21]
-    loads = [pltpu.make_async_copy(src, via, sems.at[0, k]) for k, (src, via) in enumerate(zip(ins, kept))]
-    stores = [pltpu.make_async_copy(via, dst, sems.at[1, k]) for k, (via, dst) in enumerate(zip(kept, outs))]
-    for load in loads:
-        load.start()
+    for src, dst in zip(refs[:6], refs[7:13]):
+        dst[...] = src[...]
     refs[13][...] = refs[6][0:1, :80].reshape(80)
     refs[14][...] = refs[6][1:2, :80].reshape(80)
-    for load, store in zip(loads[::-1], stores[::-1]):
-        load.wait()
-        store.start()
-    for store in stores:
-        store.wait()
 
 
 def hand_over(arrays, own):
     vm = pl.BlockSpec(memory_space=pltpu.VMEM)
-    anyspace = pl.BlockSpec(memory_space=pl.ANY)
     short = jax.ShapeDtypeStruct((80,), F32)
     return pl.pallas_call(
         copy_kernel,
         out_shape=tuple(jax.ShapeDtypeStruct(x.shape, x.dtype) for x in arrays) + (short, short),
-        in_specs=[anyspace] * 6 + [vm],
-        out_specs=[anyspace] * 6 + [vm] * 2,
-        scratch_shapes=[pltpu.VMEM(x.shape, x.dtype) for x in arrays] + [pltpu.SemaphoreType.DMA((2, 6))],
+        in_specs=[vm] * 7,
+        out_specs=[vm] * 8,
         compiler_params=pltpu.CompilerParams(vmem_limit_bytes=60 * 2**20),
         name="hand_over",
     )(*arrays, own)

time: 167 us -> 164 us (0.982)
  Pallas kernels: 166 us -> 163 us
where the time goes in v4:
time: 164 us
  Pallas kernels  163 us (99%)
    pallas_call x1, Pallas kernels, decoder_step(): pl.pallas_call(step_kernel, out_shape=(f((rows, width), F32), third, thir...  160 us

profile of v4, /device:TPU:0, one launch (start us, length us, event | category | flops | bytes accessed | tf_op | source)
XLA Modules:
  0.0 164.0 jit_solution(12100725347237574872)
XLA Ops:
  0.6 160.0 %decoder_step.1 = (f32[288,1280]{1,0:T(8,128)}, f32[2,40,640]{2,1,0:T(8,128)}, f32[2,40,640]{2,1,0:T(8,128)}, f32[2,40,640]{2,1,0:T(8,128)}, f32[40,1280]{1,0:T(...) custom-call(s32[1,304]{1,0:T(1,128)} %constant.6.cell_ref, s32[1,72]{1,0:T(1,128)} %bitcast.19, f32[72,1280]{1,0:T(8,128)} %enc_ref.1, ...), custom_call_target="tpu_custom_call" | custom-call | tf_op jit(solution)/shard_map/decoder_step/pallas_call | solution.py:626
  160.6 3.3 %hand_over.1 = (f32[288,1280]{1,0:T(8,128)}, f32[2,40,640]{2,1,0:T(8,128)}, f32[2,40,640]{2,1,0:T(8,128)}, f32[2,40,640]{2,1,0:T(8,128)}, f32[40,1280]{1,0:T(8,1...) custom-call(f32[288,1280]{1,0:T(8,128)} %get-tuple-element.23.refs_0_, f32[2,40,640]{2,1,0:T(8,128)} %get-tuple-element.24.refs_1_, ...), custom_call_target="tpu_custom_call" | custom-call | tf_op jit(solution)/shard_map/hand_over/pallas_call | solution.py:667
